TPU v7x, 256 devices: a whole 4x4x8 slice. The times are simulated.
256 devices in a mesh: dp: 64 (over z, x, y_lo), section: 4 (over y_hi, core).
Axes of the slice: x: 4, y: 4 (y_hi: 2, y_lo: 2; y = y_hi * 2 + y_lo), z: 8, core: 2. Of those that a mesh axis runs over, the one named last changes fastest.
Arguments:
- acts: bfloat16 [4, 16384, 1152], P('section', 'dp'), may hold values from -6 to 6
- grad_in: bfloat16 [4, 16384, 1152], P('section', 'dp'), may hold values from -16 to 16
- gain: float32 [4, 1152], P('section'), may hold values from 0.1 to 1.9
- w_in: bfloat16 [4, 1152, 2176], P('section', 'dp'), may hold values from -0.1875 to 0.1875
- w_out: bfloat16 [4, 1152, 2176], P('section', 'dp'), may hold values from -0.125 to 0.125
Outputs:
- handed: bfloat16 [4, 16384, 1152], P('section', 'dp')
- grad_w_in: float32 [4, 1152, 2176], P('section', 'dp')
- grad_w_out: float32 [4, 1152, 2176], P('section', 'dp')
- grad_gain: float32 [4, 1152], P('section')
All inputs are finite; a program needn't handle non-finite values.
Results may differ from a plain program's by a relative error of at most 0.0055.
Values may be sent and summed in bfloat16 or wider, within the bound.
No kernel may reach another device: no remote copies, remote signals or barrier semaphores. Data moves between devices by JAX's collectives and lax.ppermute only.
A program may use at most 128 MiB of HBM per device.

v0:
```python
import jax
import jax.numpy as jnp
from jax import lax
from jax.sharding import PartitionSpec as P

coef = 0.7978845608


def from_behind(block, axis, distance):
    devices = range(lax.axis_size(axis))
    route = [((i - distance) % len(devices), i) for i in devices]
    return lax.ppermute(block, axis, route)


def gelu_value(pre):
    inner = jnp.tanh(coef * (pre + 0.044715 * pre * pre * pre))
    return 0.5 * pre * (1.0 + inner)


def gelu_slope(pre):
    inner = jnp.tanh(coef * (pre + 0.044715 * pre * pre * pre))
    return 0.5 * (1.0 + inner) + 0.5 * pre * (1.0 - inner * inner) * coef * (
        1.0 + 0.134145 * pre * pre
    )


def token_sum(left, right):
    return lax.dot_general(
        left, right, (((0,), (0,)), ((), ())), preferred_element_type=jnp.float32
    )


def local(acts, grad_in, gain, w_in, w_out):
    source = acts[0].astype(jnp.float32)
    grad_s = grad_in[0]
    gain_s = gain[0]
    scale = 1.0 / jnp.sqrt(jnp.float32(acts.shape[1] * lax.axis_size("dp")))
    whole_in, whole_out = (
        lax.all_gather(w_in, "dp", axis=1, tiled=True),
        lax.all_gather(w_out, "dp", axis=1, tiled=True),
    )
    first = whole_in[0]
    second = whole_out[0]
    mean_row = jnp.mean(source, axis=1, keepdims=True)
    centred = source - mean_row
    inv = 1.0 / jnp.sqrt(jnp.mean(centred * centred, axis=1, keepdims=True) + 1e-06)
    normed = centred * inv
    scaled = (normed * gain_s[None, :]).astype(jnp.bfloat16)
    pre = jnp.dot(scaled, first, preferred_element_type=jnp.float32)
    hidden = gelu_value(pre).astype(jnp.bfloat16)
    out_term = token_sum(grad_s, hidden)
    dhidden = jnp.dot(grad_s, second, preferred_element_type=jnp.float32)
    dpre = (dhidden * gelu_slope(pre)).astype(jnp.bfloat16)
    in_term = token_sum(scaled, dpre)
    summed_in, summed_out = (
        lax.psum_scatter(in_term, "dp", scatter_dimension=0, tiled=True),
        lax.psum_scatter(out_term, "dp", scatter_dimension=0, tiled=True),
    )
    grad_inw = summed_in * scale
    grad_out = summed_out * scale
    dscaled = lax.dot_general(
        dpre, first, (((1,), (1,)), ((), ())), preferred_element_type=jnp.float32
    )
    grad_g = lax.psum(jnp.sum(dscaled * normed, axis=0), "dp") * scale
    dnormed = dscaled * gain_s[None, :]
    grad_x = grad_s.astype(jnp.float32) + inv * (
        dnormed
        - jnp.mean(dnormed, axis=1, keepdims=True)
        - normed * jnp.mean(dnormed * normed, axis=1, keepdims=True)
    )
    handed = from_behind(grad_x.astype(jnp.bfloat16), "section", -1)
    return (handed[None], grad_inw[None], grad_out[None], grad_g[None])


def solution(mesh):
    placed = (
        P("section", "dp", None),
        P("section", "dp", None),
        P("section", None),
        P("section", "dp", None),
        P("section", "dp", None),
    )
    return jax.shard_map(
        local,
        mesh=mesh,
        in_specs=placed,
        out_specs=(
            P("section", "dp", None),
            P("section", "dp", None),
            P("section", "dp", None),
            P("section", None),
        ),
        check_vma=False,
    )
```

profile of v0, /device:TPU:10, one launch (start us, length us, event | category | flops | bytes accessed | tf_op | source)
XLA Modules:
  0.0 1581.3 jit_solution(16029492988132432517)
XLA Ops:
  7.2 1.7 copy.18
  9.0 1.7 copy.17
  10.7 0.7 reduce.1
  11.4 1.2 convert_reduce_fusion
  12.7 1.4 fusion.34
  14.0 313.4 %all-gather.5.cloned.1.call-done = bf16[1,1152,2176]{2,0,1:T(2,128)(2,1)} async-done(((bf16[1,18,2176]{2,0,1:T(2,128)(2,1)}), bf16[1,1152,2176]{2,0,1:T(2,128)(2,1)}) %all-gather.5.cloned.1.call-update) | async-done | bytes 5013520 | tf_op jit(solution)/shard_map/all_gather | solution.py:39
  327.4 5.9 fusion.2
  333.3 5.8 convolution_bitcast_fusion
  339.1 12.3 copy.19
  351.5 293.3 %all-gather.3.cloned.1.call-done = bf16[1,1152,2176]{2,0,1:T(2,128)(2,1)} async-done(((bf16[1,18,2176]{2,0,1:T(2,128)(2,1)}), bf16[1,1152,2176]{2,0,1:T(2,128)(2,1)}) %all-gather.3.cloned.1.call-update) | async-done | bytes 5013520 | tf_op jit(solution)/shard_map/all_gather | solution.py:40
  644.8 6.3 fusion.10
  651.1 1.0 copy-done.2
  652.1 5.4 fusion.44
  657.6 1.2 copy-done.3
  658.8 5.8 fusion.33
  664.7 0.5 fusion.31
  665.3 0.6 dynamic-slice
  666.6 186.4 %psum.7 = f32[1152]{0:T(1024)S(1)} all-reduce(f32[1152]{0:T(1024)S(1)} %get-tuple-element.16), channel_id=1, replica_groups=mesh['dp'=64,'section'=4] {'dp'}, use_global_device_ids=true, to_apply=%region_7.0 | all-reduce | flops 1152 | bytes 9216 | tf_op jit(solution)/shard_map/psum | solution.py:64
  853.0 0.6 broadcast_in_dim.19
  853.6 717.7 %all-reduce.5.cloned.1.call-done = (f32[1152,2176]{1,0:T(8,128)}, f32[1152,2176]{1,0:T(8,128)}) async-done(((f32[1152,2176]{1,0:T(8,128)}, f32[1152,2176]{1,0:T(8,128)}), (f32[1152,2176]{1,0:T(8,128)}, f32[1152,2176]{1,0:T(8,128)})) %all-reduce.5.cloned.1.call-update) | async-done | bytes 20054032
  1571.2 1.1 fusion.54
  1572.3 0.8 copy.21
  1573.1 0.8 copy.20
  1574.0 0.8 copy.45
  (20 shorter events, 0.3 us)
Async XLA Ops:
  7.2 320.2 %all-gather.5.cloned.1.call-start = ((), (), s32[]{:S(2)}) async-start(), calls=%async_computation.1 | async-start | bytes 10183680 | tf_op jit(solution)/shard_map/all_gather | solution.py:39
  8.9 635.9 %all-gather.3.cloned.1.call-start = ((), (), s32[]{:S(2)}) async-start(), calls=%async_computation | async-start | bytes 10183680 | tf_op jit(solution)/shard_map/all_gather | solution.py:40
  10.7 1560.6 %all-reduce.5.cloned.1.call-start = ((), (), s32[]{:S(2)}) async-start(), calls=%async_computation.2 | async-start | bytes 40108032
  14.0 319.3 %copy-start.1 = (bf16[1,256,1152]{2,1,0:T(8,128)(2,1)S(1)}, bf16[1,256,1152]{2,1,0:T(8,128)(2,1)}, u32[]{:S(2)}) copy-start(bf16[1,256,1152]{2,1,0:T(8,128)(2,1)} %param.6) | copy-start | bytes 1769476
  351.5 300.6 %copy-start = (bf16[1,256,1152]{2,1,0:T(8,128)(2,1)S(1)}, bf16[1,256,1152]{2,1,0:T(8,128)(2,1)}, u32[]{:S(2)}) copy-start(bf16[1,256,1152]{2,1,0:T(8,128)(2,1)} %param.5) | copy-start | bytes 1769476
  651.1 1.0 copy-start.2
  657.6 1.2 copy-start.3
  664.6 0.7 copy-start.4
  665.2 188.4 %collective-permute-start = (bf16[256,1152]{1,0:T(8,128)(2,1)S(1)}, bf16[256,1152]{1,0:T(8,128)(2,1)S(1)}, u32[]{:S(2)}, u32[]{:S(2)}) collective-permute-start(bf16[256,1152]{1,0:T(8,128)(2,1)S(1)} %fusion.31), channel_id=1, source_target_pairs={{1,0},{2,1},{3,2},{0,3},{5,4},{6,5},{7,6},{4,7},{9,8},{10,9},{11,1... | collective-permute-start | bytes 1769480 | tf_op jit(solution)/shard_map/ppermute | solution.py:12
Sparse Core Ops, SparseCore 0:
  10.4 316.9 all-gather.4
  329.8 315.0 all-gather.2
  657.7 913.4 all-reduce.4
where the time goes:
time: 1590 us; the launch traced here: 1580 us
  waiting for transfers between devices  1320 us (83%)
  blocking collectives  186 us (12%)
  matrix products  29.3 us (2%)
  local copies, waits for them, and re-layouts  21.6 us (1%)
    unnamed x4, waiting for transfers between devices  718 us
    all_gather x1, waiting for transfers between devices, local(): lax.all_gather(w_in, 'dp', axis=1, tiled=True)  313 us
    all_gather x1, waiting for transfers between devices, local(): lax.all_gather(w_out, 'dp', axis=1, tiled=True)  293 us
    psum x1, blocking collectives, local(): grad_g = lax.psum(jnp.sum(dscaled * normed, axis=0), 'dp') * scale  186 us
  transfers between devices with their start and end apart: 4, of which 3 were waited for; matrix products, arithmetic and copies ran while one was open for 2% of the time, Pallas kernels for 0%

commit v1 on v0

v1 whole, which is shorter than its diff:
```python
import jax
import jax.numpy as jnp
from jax import lax
from jax.sharding import Mesh, PartitionSpec as P

coef = 0.7978845608
f32, bf16 = jnp.float32, jnp.bfloat16


def shift(block, axis, distance):
    size = lax.axis_size(axis)
    return lax.ppermute(block, axis, [(i, (i + distance) % size) for i in range(size)])


SWAP = [(2 * y + c, 2 * c + y) for y in range(2) for c in range(2)]
OUT_CROSS = [(2 * y + c, 2 * c + 1 - y) for y in range(2) for c in range(2)]
BACK_CROSS = [(b, a) for a, b in OUT_CROSS]


def pick(flag, a, b):
    return jnp.where(flag == 0, a, b), jnp.where(flag == 0, b, a)


def direct_gather(block, axis):
    size = lax.axis_size(axis)
    me = lax.axis_index(axis)
    out = jnp.zeros((size,) + block.shape, block.dtype)
    out = lax.dynamic_update_index_in_dim(out, block, me, 0)
    for k in range(1, size):
        got = shift(block, axis, k)
        out = lax.dynamic_update_index_in_dim(out, got, (me - k) % size, 0)
    return out


def direct_scatter(blocks, axis):
    size = lax.axis_size(axis)
    me = lax.axis_index(axis)
    total = lax.dynamic_index_in_dim(blocks, me, 0, keepdims=False).astype(f32)
    for k in range(1, size):
        part = lax.dynamic_index_in_dim(blocks, (me + k) % size, 0, keepdims=False)
        total = total + shift(part, axis, k).astype(f32)
    return total


def dot(a, b, ca, cb):
    return lax.dot_general(a, b, (((ca,), (cb,)), ((), ())), preferred_element_type=f32)


def local(nz, nx, acts, grad_in, gain, w_in, w_out):
    y, c = lax.axis_index("y"), lax.axis_index("c")
    rows, hid = w_in.shape[1:]
    half = hid // 2
    d = acts.shape[2]
    tokens = acts.shape[1]
    scale = 1.0 / jnp.sqrt(jnp.float32(tokens * nz * nx * 2))

    both = jnp.concatenate([w_in, w_out], axis=0)
    low, high = both[:, :, :half], both[:, :, half:]
    same, cross = pick(y, low, high)
    same = lax.ppermute(same, ("y", "c"), SWAP)
    cross = lax.ppermute(cross, ("y", "c"), OUT_CROSS)
    top, bottom = pick(c, same, cross)
    shard = jnp.concatenate([top, bottom], axis=1)
    first = direct_gather(shard[0], "x").reshape(nx * 2 * rows, half)
    first = lax.all_gather(first, "z", axis=0, tiled=True)
    second = lax.all_gather(shard[1], "z", axis=0, tiled=False)
    second = direct_gather(second, "x")
    second = second.transpose(1, 0, 2, 3).reshape(d, half)

    acts_s = lax.ppermute(acts[0], ("y", "c"), SWAP)
    grad_own = lax.ppermute(grad_in[0], ("y", "c"), SWAP)
    gain_s = lax.ppermute(gain[0], ("y", "c"), SWAP)
    source = acts_s.astype(f32)
    centred = source - jnp.mean(source, axis=1, keepdims=True)
    inv = 1.0 / jnp.sqrt(jnp.mean(centred * centred, axis=1, keepdims=True) + 1e-06)
    normed = centred * inv
    scaled_own = (normed * gain_s[None, :]).astype(bf16)
    scaled = jnp.concatenate([scaled_own, shift(scaled_own, "c", 1)], axis=0)
    grads = jnp.concatenate([grad_own, shift(grad_own, "c", 1)], axis=0)

    pre = dot(scaled, first, 1, 0)
    th = jnp.tanh(coef * (pre + 0.044715 * pre * pre * pre))
    hidden = (0.5 * pre * (1.0 + th)).astype(bf16)
    slope = 0.5 * (1.0 + th) + 0.5 * pre * (1.0 - th * th) * coef * (
        1.0 + 0.134145 * pre * pre
    )
    out_term = dot(grads, hidden, 0, 0).astype(bf16)
    sum_out = lax.psum_scatter(out_term, "z", scatter_dimension=0, tiled=True)
    sum_out = direct_scatter(sum_out.reshape(nx, 2 * rows, half), "x")

    dpre = (dot(grads, second, 1, 0) * slope).astype(bf16)
    in_term = dot(scaled, dpre, 0, 0).astype(bf16)
    in_term = in_term.reshape(nz, nx, 2 * rows, half).transpose(1, 0, 2, 3)
    sum_in = direct_scatter(in_term, "x").astype(bf16)
    sum_in = lax.all_to_all(sum_in, "z", 0, 0)
    sum_in = jnp.sum(sum_in.astype(f32), axis=0)

    sums = jnp.stack([sum_in, sum_out]) * scale
    same, cross = pick(c, sums[:, :rows], sums[:, rows:])
    same = lax.ppermute(same, ("y", "c"), SWAP)
    cross = lax.ppermute(cross, ("y", "c"), BACK_CROSS)
    low, high = pick(y, same, cross)
    grad_w = jnp.concatenate([low, high], axis=2)

    partial = dot(dpre, first, 1, 1)
    dscaled = partial[:tokens] + shift(partial[tokens:], "c", 1)
    grad_g = lax.psum(jnp.sum(dscaled * normed, axis=0), ("z", "x", "c")) * scale
    grad_g = lax.ppermute(grad_g, ("y", "c"), SWAP)
    dnormed = dscaled * gain_s[None, :]
    grad_x = grad_own.astype(f32) + inv * (
        dnormed
        - jnp.mean(dnormed, axis=1, keepdims=True)
        - normed * jnp.mean(dnormed * normed, axis=1, keepdims=True)
    )
    route = []
    for yy in range(2):
        for hh in range(2):
            for cc in range(2):
                to = (2 * hh + yy - 1) % 4
                route.append((4 * yy + 2 * hh + cc, 4 * cc + 2 * (to // 2) + to % 2))
    handed = lax.ppermute(grad_x.astype(bf16), ("y", "h", "c"), route)
    return handed[None], grad_w[0][None], grad_w[1][None], grad_g[None]


def solution(mesh):
    nz, nx = 8, mesh.shape["dp"] // 16
    fine = Mesh(mesh.devices.reshape(nz, nx, 2, 2, 2), ("z", "x", "y", "h", "c"))
    wide = P(("h", "c"), ("z", "x", "y"), None)
    slim = P(("h", "c"), None)

    def run(*args):
        return local(nz, nx, *args)

    return jax.shard_map(
        run,
        mesh=fine,
        in_specs=(wide, wide, slim, wide, wide),
        out_specs=(wide, wide, wide, slim),
        check_vma=False,
    )
```

time: 1590 us -> 326 us (0.21)
  waiting for transfers between devices: 1320 us -> 43.8 us
  starting transfers between devices: 0.21 us -> 56.2 us
  blocking collectives: 186 us -> 155 us
    unnamed x4 -> x2, waiting for transfers between devices: 718 us -> 0.03 us
    all_gather x2 -> x1, waiting for transfers between devices: 607 us -> 0.01 us  [local(): first = lax.all_gather(first, 'z', axis=0, tiled=True)]
    psum x1, blocking collectives: 186 us -> 125 us  [local(): lax.psum(jnp.sum(dscaled * normed, axis=0), ('z', 'x', 'c')) * scale]
    ppermute x1 -> x24, starting transfers between devices: 0.08 us -> 51 us  [the longest x15 23.8 us: shift(): lax.ppermute(block, axis, [(i, (i + distance) % size) for i in range(size)])]
    ppermute x1 -> x24, waiting for transfers between devices: 0.01 us -> 43.8 us  [the longest x15 37.3 us: shift(): lax.ppermute(block, axis, [(i, (i + distance) % size) for i in range(size)])]
    all_gather x0 -> x1, blocking collectives: none -> 30.2 us  [local(): second = lax.all_gather(shard[1], 'z', axis=0, tiled=False)]
  transfers between devices with their start and end apart: 4 -> 27, of which waited for: 3 -> 9; matrix products, arithmetic and copies ran while one was open for 2% -> 13% of each run, Pallas kernels for 0% -> 0%
where the time goes in v1:
time: 326 us; the launch traced here: 320 us
  blocking collectives  155 us (48%)
  starting transfers between devices  56.2 us (17%)
  waiting for transfers between devices  43.8 us (13%)
  local copies, waits for them, and re-layouts  27.7 us (8%)
  matrix products  17.5 us (5%)
  between operations  14.6 us (4%)
  other arithmetic  5.68 us (2%)
    psum x1, blocking collectives, local(): lax.psum(jnp.sum(dscaled * normed, axis=0), ('z', 'x', 'c')) * scale  125 us
    ppermute x15, waiting for transfers between devices, shift(): lax.ppermute(block, axis, [(i, (i + distance) % size) for i in range(size)])  37.3 us
    all_gather x1, blocking collectives, local(): second = lax.all_gather(shard[1], 'z', axis=0, tiled=False)  30.2 us
    ppermute x15, starting transfers between devices, shift(): lax.ppermute(block, axis, [(i, (i + distance) % size) for i in range(size)])  23.8 us
    dot_general x5, matrix products, dot(): lax.dot_general(a, b, (((ca,), (cb,)), ((), ())), preferred_element_type=...  17.5 us
    ppermute x1, starting transfers between devices, local(): handed = lax.ppermute(grad_x.astype(bf16), ('y', 'h', 'c'), route)  8.86 us
    ppermute x2, starting transfers between devices, local(): same = lax.ppermute(same, ('y', 'c'), SWAP)  8.11 us
    unnamed x25, local copies, waits for them, and re-layouts  8.03 us
  transfers between devices with their start and end apart: 27, of which 9 were waited for; matrix products, arithmetic and copies ran while one was open for 13% of the time, Pallas kernels for 0%

profile of v1, /device:TPU:10, one launch (start us, length us, event | category | flops | bytes accessed | tf_op | source)
XLA Modules:
  0.0 320.4 jit_solution(10516157296994219645)
XLA Ops:
  9.7 2.6 collective-permute-start.3
  12.3 3.4 %collective-permute-done.3 = bf16[2,18,1088]{2,1,0:T(8,128)(2,1)S(1)} collective-permute-done((bf16[2,18,1088]{2,1,0:T(8,128)(2,1)S(1)}, bf16[2,18,1088]{2,1,0:T(8,128)(2,1)S(1)}, u32[]{:S(2)}, u32[]{:S(2)}) %collective-permute-start.3) | collective-permute-done | bytes 78368 | tf_op jit(solution)/shard_map/ppermute | solution.py:60
  17.4 2.8 collective-permute-start.11
  20.8 2.7 collective-permute-done.11
  27.9 3.4 %collective-permute-start = (bf16[256,1152]{1,0:T(8,128)(2,1)}, bf16[256,1152]{1,0:T(8,128)(2,1)}, u32[]{:S(2)}, u32[]{:S(2)}) collective-permute-start(bf16[256,1152]{1,0:T(8,128)(2,1)} %bitcast), channel_id=1, source_target_pairs={{0,0},{1,4},{4,1},{5,5},{2,2},{3,6},{6,3},{7,7},{8,8},{9,12},{12,9... | collective-permute-start | bytes 1769480 | tf_op jit(solution)/shard_map/ppermute | solution.py:71
  34.2 30.2 %all_gather.6 = bf16[8,36,1088]{2,1,0:T(8,128)(2,1)S(1)} all-gather(bf16[1,36,1088]{2,1,0:T(8,128)(2,1)S(1)} %get-tuple-element.39), channel_id=1, replica_groups=mesh['z'=8,'x'=4,'y'=2,'h'=2,'c'=2] {'z'}, dimensions={0}, use_global_device_ids=true | all-gather | bytes 705024 | tf_op jit(solution)/shard_map/all_gather | solution.py:66
  73.6 8.1 %collective-permute-done.5 = bf16[8,36,1088]{2,0,1:T(8,128)(2,1)S(1)} collective-permute-done((bf16[8,36,1088]{2,0,1:T(8,128)(2,1)}, bf16[8,36,1088]{2,0,1:T(8,128)(2,1)S(1)}, u32[]{:S(2)}, u32[]{:S(2)}) %collective-permute-start.5) | collective-permute-done | bytes 626720 | tf_op jit(solution)/shard_map/ppermute | solution.py:12
  82.9 3.9 %fusion.27 = f32[512,1088]{0,1:T(8,128)S(1)} fusion(bf16[1152,1088]{1,0:T(8,128)(2,1)} %all-gather.2.cloned.1.call-done, bf16[256,1152]{1,0:T(8,128)(2,1)} %collective-permute-done.9, bf16[256,1152]{1,0:T(8,128)(2,1)} %copy-done.1), kind=kOutput, calls=%fused_computation.40 | convolution fusion | flops 1285816320 | bytes 5914624 | tf_op jit(solution)/shard_map/dot_general | solution.py:46
  88.2 3.4 %convolution_convert_fusion.1 = bf16[1152,1088]{1,0:T(8,128)(2,1)} fusion(bf16[512,1152]{1,0:T(8,128)(2,1)S(1)} %copy-done.4, f32[512,1088]{0,1:T(8,128)S(1)} %fusion.27), kind=kOutput, calls=%fused_computation.1 | convolution fusion | flops 1289723904 | bytes 5914624 | tf_op jit(solution)/shard_map/dot_general | solution.py:46
  94.1 2.5 reshape.54
  96.7 5.6 %fusion = bf16[512,1088]{0,1:T(8,128)(2,1)S(1)} fusion(bf16[512,1152]{1,0:T(8,128)(2,1)} %copy-done.3, bf16[1152,1088]{1,0:T(8,128)(2,1)} %reshape.54, f32[512,1088]{0,1:T(8,128)} %copy-done.9), kind=kOutput, calls=%fused_computation.5 | convolution fusion | flops 1294041088 | bytes 7028736 | tf_op jit(solution)/shard_map/dot_general | solution.py:46
  103.3 2.7 convolution_convert_fusion
  106.0 3.3 %copy.64 = bf16[1152,1088]{1,0:T(8,128)(2,1)} copy(bf16[1152,1088]{0,1:T(8,128)(2,1)S(1)} %convolution_convert_fusion) | data formatting | bytes 5013504 | tf_op jit(solution)/shard_map/convert_element_type | solution.py:92
  109.3 3.9 %reshape.56 = bf16[8,4,36,1088]{3,2,1,0:T(8,128)(2,1)S(1)} reshape(bf16[1152,1088]{1,0:T(8,128)(2,1)} %copy.64) | data formatting | bytes 5013504 | tf_op jit(solution)/shard_map/reshape | solution.py:93
  113.6 3.3 %collective-permute-start.17 = (bf16[8,36,1088]{2,0,1:T(8,128)(2,1)S(1)}, bf16[8,36,1088]{2,0,1:T(8,128)(2,1)S(1)}, u32[]{:S(2)}, u32[]{:S(2)}) collective-permute-start(bf16[8,36,1088]{2,0,1:T(8,128)(2,1)S(1)} %bitcast.55), channel_id=1, source_target_pairs={{0,24},{8,0},{16,8},{24,16},{1,25},{9,1},{17,9},{25,17},{2,26},{10... | collective-permute-start | bytes 1880072 | tf_op jit(solution)/shard_map/ppermute | solution.py:12
  117.1 2.3 collective-permute-start.15
  122.6 18.8 %collective-permute-done.17 = bf16[8,36,1088]{2,0,1:T(8,128)(2,1)S(1)} collective-permute-done((bf16[8,36,1088]{2,0,1:T(8,128)(2,1)S(1)}, bf16[8,36,1088]{2,0,1:T(8,128)(2,1)S(1)}, u32[]{:S(2)}, u32[]{:S(2)}) %collective-permute-start.17) | collective-permute-done | bytes 626720 | tf_op jit(solution)/shard_map/ppermute | solution.py:12
  144.6 5.1 %all-to-all-start = ((bf16[8,36,1088]{2,1,0:T(8,128)(2,1)}), bf16[8,36,1088]{2,1,0:T(8,128)(2,1)S(1)}, u32[]{:S(2)}, u32[]{:S(2)}) async-start(bf16[8,36,1088]{2,1,0:T(8,128)(2,1)} %copy.69), calls=%async_computation | async-start | bytes 1474560 | tf_op jit(solution)/shard_map/all_to_all | solution.py:95
  153.2 8.9 %collective-permute-start.14 = (bf16[256,1152]{1,0:T(8,128)(2,1)S(1)}, bf16[256,1152]{1,0:T(8,128)(2,1)S(1)}, u32[]{:S(2)}, u32[]{:S(2)}) collective-permute-start(bf16[256,1152]{1,0:T(8,128)(2,1)S(1)} %fusion.20), channel_id=1, source_target_pairs={{0,3},{1,7},{2,1},{3,5},{4,0},{5,4},{6,2},{7,6},{8,11},{9,15},{10,... | collective-permute-start | bytes 1769480 | tf_op jit(solution)/shard_map/ppermute | solution.py:121
  162.1 124.7 %psum.7 = f32[1152]{0:T(1024)S(1)} all-reduce(f32[1152]{0:T(1024)S(1)} %get-tuple-element.20), channel_id=1, replica_groups=mesh['z'=8,'x'=4,'y'=2,'h'=2,'c'=2] {'z','x','c'}, use_global_device_ids=true, to_apply=%region_7.8 | all-reduce | flops 1152 | bytes 9216 | tf_op jit(solution)/shard_map/psum | solution.py:107
  287.9 5.7 %collective-permute-start.20 = (bf16[36,1088]{1,0:T(8,128)(2,1)S(1)}, bf16[36,1088]{1,0:T(8,128)(2,1)S(1)}, u32[]{:S(2)}, u32[]{:S(2)}) collective-permute-start(bf16[36,1088]{1,0:T(8,128)(2,1)S(1)} %get-tuple-element.35), channel_id=1, source_target_pairs={{0,24},{8,0},{16,8},{24,16},{1,25},{9,1},{17,9},{25,17},{2,26},{10... | collective-permute-start | bytes 235016 | tf_op jit(solution)/shard_map/ppermute | solution.py:12
  295.7 3.9 %collective-permute-done.19 = bf16[36,1088]{1,0:T(8,128)(2,1)S(1)} collective-permute-done((bf16[36,1088]{1,0:T(8,128)(2,1)S(1)}, bf16[36,1088]{1,0:T(8,128)(2,1)S(1)}, u32[]{:S(2)}, u32[]{:S(2)}) %collective-permute-start.19) | collective-permute-done | bytes 78368 | tf_op jit(solution)/shard_map/ppermute | solution.py:12
  299.9 5.5 %collective-permute-start.21 = (f32[2,18,1088]{2,1,0:T(8,128)S(1)}, f32[2,18,1088]{2,1,0:T(8,128)S(1)}, u32[]{:S(2)}, u32[]{:S(2)}) collective-permute-start(f32[2,18,1088]{2,1,0:T(8,128)S(1)} %get-tuple-element.33), channel_id=1, source_target_pairs={{0,0},{1,4},{4,1},{5,5},{2,2},{3,6},{6,3},{7,7},{8,8},{9,12},{12,9... | collective-permute-start | bytes 470024 | tf_op jit(solution)/shard_map/ppermute | solution.py:100
  307.3 3.0 collective-permute-done.23
  (109 shorter events, 46.1 us)
Async XLA Ops:
  7.2 75.8 %all-gather.2.cloned.1.call-start = ((), (), s32[]{:S(2)}) async-start(), calls=%async_computation.2 | async-start | bytes 2985984 | tf_op jit(solution)/shard_map/all_gather | solution.py:65
  9.7 6.1 %collective-permute-start.3 = (bf16[2,18,1088]{2,1,0:T(8,128)(2,1)S(1)}, bf16[2,18,1088]{2,1,0:T(8,128)(2,1)S(1)}, u32[]{:S(2)}, u32[]{:S(2)}) collective-permute-start(bf16[2,18,1088]{2,1,0:T(8,128)(2,1)S(1)} %get-tuple-element.43), channel_id=1, source_target_pairs={{0,0},{1,4},{4,1},{5,5},{2,2},{3,6},{6,3},{7,7},{8,8},{9,12},{12,9... | collective-permute-start | bytes 235016 | tf_op jit(solution)/shard_map/ppermute | solution.py:60
  17.4 6.1 %collective-permute-start.11 = (bf16[36,1088]{1,0:T(8,128)(2,1)S(1)}, bf16[36,1088]{1,0:T(8,128)(2,1)S(1)}, u32[]{:S(2)}, u32[]{:S(2)}) collective-permute-start(bf16[36,1088]{1,0:T(8,128)(2,1)S(1)} %get-tuple-element.37), channel_id=1, source_target_pairs={{0,16},{8,24},{16,0},{24,8},{1,17},{9,25},{17,1},{25,9},{2,18},{10... | collective-permute-start | bytes 235016 | tf_op jit(solution)/shard_map/ppermute | solution.py:12
  25.7 261.1 %reduce-scatter.2.cloned.1.call-start = ((), (), s32[]{:S(2)}) async-start(), calls=%async_computation.3 | async-start | bytes 2985984 | tf_op jit(solution)/shard_map/reduce_scatter | solution.py:88
  25.8 43.1 %collective-permute-start.1 = (bf16[256,1152]{1,0:T(8,128)(2,1)}, bf16[256,1152]{1,0:T(8,128)(2,1)S(1)}, u32[]{:S(2)}, u32[]{:S(2)}) collective-permute-start(bf16[256,1152]{1,0:T(8,128)(2,1)} %bitcast.1), channel_id=1, source_target_pairs={{0,0},{1,4},{4,1},{5,5},{2,2},{3,6},{6,3},{7,7},{8,8},{9,12},{12,9... | collective-permute-start | bytes 1769480 | tf_op jit(solution)/shard_map/ppermute | solution.py:70
  27.9 44.1 %collective-permute-start = (bf16[256,1152]{1,0:T(8,128)(2,1)}, bf16[256,1152]{1,0:T(8,128)(2,1)}, u32[]{:S(2)}, u32[]{:S(2)}) collective-permute-start(bf16[256,1152]{1,0:T(8,128)(2,1)} %bitcast), channel_id=1, source_target_pairs={{0,0},{1,4},{4,1},{5,5},{2,2},{3,6},{6,3},{7,7},{8,8},{9,12},{12,9... | collective-permute-start | bytes 1769480 | tf_op jit(solution)/shard_map/ppermute | solution.py:71
  32.0 39.6 %collective-permute-start.8 = (f32[1152]{0:T(1024)}, f32[1152]{0:T(1024)S(1)}, u32[]{:S(2)}, u32[]{:S(2)}) collective-permute-start(f32[1152]{0:T(1024)} %reduce), channel_id=1, source_target_pairs={{0,0},{1,4},{4,1},{5,5},{2,2},{3,6},{6,3},{7,7},{8,8},{9,12},{12,9... | collective-permute-start | bytes 13832 | tf_op jit(solution)/shard_map/ppermute | solution.py:72
  65.3 16.4 %collective-permute-start.5 = (bf16[8,36,1088]{2,0,1:T(8,128)(2,1)}, bf16[8,36,1088]{2,0,1:T(8,128)(2,1)S(1)}, u32[]{:S(2)}, u32[]{:S(2)}) collective-permute-start(bf16[8,36,1088]{2,0,1:T(8,128)(2,1)} %copy.58), channel_id=1, source_target_pairs={{0,8},{8,16},{16,24},{24,0},{1,9},{9,17},{17,25},{25,1},{2,10},{10... | collective-permute-start | bytes 1880072 | tf_op jit(solution)/shard_map/ppermute | solution.py:12
  66.4 25.3 %collective-permute-start.6 = (bf16[8,36,1088]{2,0,1:T(8,128)(2,1)}, bf16[8,36,1088]{2,0,1:T(8,128)(2,1)}, u32[]{:S(2)}, u32[]{:S(2)}) collective-permute-start(bf16[8,36,1088]{2,0,1:T(8,128)(2,1)} %copy.58), channel_id=1, source_target_pairs={{0,16},{8,24},{16,0},{24,8},{1,17},{9,25},{17,1},{25,9},{2,18},{10... | collective-permute-start | bytes 1880072 | tf_op jit(solution)/shard_map/ppermute | solution.py:12
  68.8 24.0 %collective-permute-start.7 = (bf16[8,36,1088]{2,0,1:T(8,128)(2,1)}, bf16[8,36,1088]{2,0,1:T(8,128)(2,1)}, u32[]{:S(2)}, u32[]{:S(2)}) collective-permute-start(bf16[8,36,1088]{2,0,1:T(8,128)(2,1)} %copy.58), channel_id=1, source_target_pairs={{0,24},{8,0},{16,8},{24,16},{1,25},{9,1},{17,9},{25,17},{2,26},{10... | collective-permute-start | bytes 1880072 | tf_op jit(solution)/shard_map/ppermute | solution.py:12
  71.9 11.1 %collective-permute-start.9 = (bf16[256,1152]{1,0:T(8,128)(2,1)S(1)}, bf16[256,1152]{1,0:T(8,128)(2,1)}, u32[]{:S(2)}, u32[]{:S(2)}) collective-permute-start(bf16[256,1152]{1,0:T(8,128)(2,1)S(1)} %fusion.15), channel_id=1, source_target_pairs={{0,1},{1,0},{2,3},{3,2},{4,5},{5,4},{6,7},{7,6},{8,9},{9,8},{10,11... | collective-permute-start | bytes 1769480 | tf_op jit(solution)/shard_map/ppermute | solution.py:12
  72.0 9.8 %collective-permute-start.2 = (bf16[256,1152]{1,0:T(8,128)(2,1)}, bf16[256,1152]{1,0:T(8,128)(2,1)S(1)}, u32[]{:S(2)}, u32[]{:S(2)}) collective-permute-start(bf16[256,1152]{1,0:T(8,128)(2,1)} %collective-permute-done), channel_id=1, source_target_pairs={{0,1},{1,0},{2,3},{3,2},{4,5},{5,4},{6,7},{7,6},{8,9},{9,8},{10,11... | collective-permute-start | bytes 1769480 | tf_op jit(solution)/shard_map/ppermute | solution.py:12
  113.6 27.8 %collective-permute-start.17 = (bf16[8,36,1088]{2,0,1:T(8,128)(2,1)S(1)}, bf16[8,36,1088]{2,0,1:T(8,128)(2,1)S(1)}, u32[]{:S(2)}, u32[]{:S(2)}) collective-permute-start(bf16[8,36,1088]{2,0,1:T(8,128)(2,1)S(1)} %bitcast.55), channel_id=1, source_target_pairs={{0,24},{8,0},{16,8},{24,16},{1,25},{9,1},{17,9},{25,17},{2,26},{10... | collective-permute-start | bytes 1880072 | tf_op jit(solution)/shard_map/ppermute | solution.py:12
  116.9 24.5 %collective-permute-start.16 = (bf16[8,36,1088]{2,0,1:T(8,128)(2,1)S(1)}, bf16[8,36,1088]{2,0,1:T(8,128)(2,1)S(1)}, u32[]{:S(2)}, u32[]{:S(2)}) collective-permute-start(bf16[8,36,1088]{2,0,1:T(8,128)(2,1)S(1)} %bitcast.56), channel_id=1, source_target_pairs={{0,16},{8,24},{16,0},{24,8},{1,17},{9,25},{17,1},{25,9},{2,18},{10... | collective-permute-start | bytes 1880072 | tf_op jit(solution)/shard_map/ppermute | solution.py:12
  117.1 26.3 %collective-permute-start.15 = (bf16[8,36,1088]{2,0,1:T(8,128)(2,1)S(1)}, bf16[8,36,1088]{2,0,1:T(8,128)(2,1)S(1)}, u32[]{:S(2)}, u32[]{:S(2)}) collective-permute-start(bf16[8,36,1088]{2,0,1:T(8,128)(2,1)S(1)} %bitcast.57), channel_id=1, source_target_pairs={{0,8},{8,16},{16,24},{24,0},{1,9},{9,17},{17,25},{25,1},{2,10},{10... | collective-permute-start | bytes 1880072 | tf_op jit(solution)/shard_map/ppermute | solution.py:12
  122.6 27.1 %collective-permute-start.13 = (f32[256,1152]{1,0:T(8,128)}, f32[256,1152]{1,0:T(8,128)S(1)}, u32[]{:S(2)}, u32[]{:S(2)}) collective-permute-start(f32[256,1152]{1,0:T(8,128)} %slice.45), channel_id=1, source_target_pairs={{0,1},{1,0},{2,3},{3,2},{4,5},{5,4},{6,7},{7,6},{8,9},{9,8},{10,11... | collective-permute-start | bytes 3538952 | tf_op jit(solution)/shard_map/ppermute | solution.py:12
  144.6 150.5 %all-to-all-start = ((bf16[8,36,1088]{2,1,0:T(8,128)(2,1)}), bf16[8,36,1088]{2,1,0:T(8,128)(2,1)S(1)}, u32[]{:S(2)}, u32[]{:S(2)}) async-start(bf16[8,36,1088]{2,1,0:T(8,128)(2,1)} %copy.69), calls=%async_computation | async-start | bytes 1474560 | tf_op jit(solution)/shard_map/all_to_all | solution.py:95
  153.2 157.7 %collective-permute-start.14 = (bf16[256,1152]{1,0:T(8,128)(2,1)S(1)}, bf16[256,1152]{1,0:T(8,128)(2,1)S(1)}, u32[]{:S(2)}, u32[]{:S(2)}) collective-permute-start(bf16[256,1152]{1,0:T(8,128)(2,1)S(1)} %fusion.20), channel_id=1, source_target_pairs={{0,3},{1,7},{2,1},{3,5},{4,0},{5,4},{6,2},{7,6},{8,11},{9,15},{10,... | collective-permute-start | bytes 1769480 | tf_op jit(solution)/shard_map/ppermute | solution.py:121
  287.9 7.9 %collective-permute-start.20 = (bf16[36,1088]{1,0:T(8,128)(2,1)S(1)}, bf16[36,1088]{1,0:T(8,128)(2,1)S(1)}, u32[]{:S(2)}, u32[]{:S(2)}) collective-permute-start(bf16[36,1088]{1,0:T(8,128)(2,1)S(1)} %get-tuple-element.35), channel_id=1, source_target_pairs={{0,24},{8,0},{16,8},{24,16},{1,25},{9,1},{17,9},{25,17},{2,26},{10... | collective-permute-start | bytes 235016 | tf_op jit(solution)/shard_map/ppermute | solution.py:12
  293.6 6.1 %collective-permute-start.19 = (bf16[36,1088]{1,0:T(8,128)(2,1)S(1)}, bf16[36,1088]{1,0:T(8,128)(2,1)S(1)}, u32[]{:S(2)}, u32[]{:S(2)}) collective-permute-start(bf16[36,1088]{1,0:T(8,128)(2,1)S(1)} %get-tuple-element.36), channel_id=1, source_target_pairs={{0,16},{8,24},{16,0},{24,8},{1,17},{9,25},{17,1},{25,9},{2,18},{10... | collective-permute-start | bytes 235016 | tf_op jit(solution)/shard_map/ppermute | solution.py:12
  293.6 6.1 %collective-permute-start.18 = (bf16[36,1088]{1,0:T(8,128)(2,1)S(1)}, bf16[36,1088]{1,0:T(8,128)(2,1)S(1)}, u32[]{:S(2)}, u32[]{:S(2)}) collective-permute-start(bf16[36,1088]{1,0:T(8,128)(2,1)S(1)} %get-tuple-element.34), channel_id=1, source_target_pairs={{0,8},{8,16},{16,24},{24,0},{1,9},{9,17},{17,25},{25,1},{2,10},{10... | collective-permute-start | bytes 235016 | tf_op jit(solution)/shard_map/ppermute | solution.py:12
  299.8 11.2 %collective-permute-start.22 = (f32[2,18,1088]{2,1,0:T(8,128)S(1)}, f32[2,18,1088]{2,1,0:T(8,128)S(1)}, u32[]{:S(2)}, u32[]{:S(2)}) collective-permute-start(f32[2,18,1088]{2,1,0:T(8,128)S(1)} %get-tuple-element.32), channel_id=1, source_target_pairs={{1,0},{5,1},{0,4},{4,5},{3,2},{7,3},{2,6},{6,7},{9,8},{13,9},{8,12... | collective-permute-start | bytes 470024 | tf_op jit(solution)/shard_map/ppermute | solution.py:101
  299.9 11.1 %collective-permute-start.21 = (f32[2,18,1088]{2,1,0:T(8,128)S(1)}, f32[2,18,1088]{2,1,0:T(8,128)S(1)}, u32[]{:S(2)}, u32[]{:S(2)}) collective-permute-start(f32[2,18,1088]{2,1,0:T(8,128)S(1)} %get-tuple-element.33), channel_id=1, source_target_pairs={{0,0},{1,4},{4,1},{5,5},{2,2},{3,6},{6,3},{7,7},{8,8},{9,12},{12,9... | collective-permute-start | bytes 470024 | tf_op jit(solution)/shard_map/ppermute | solution.py:100
  305.4 5.0 %collective-permute-start.23 = (f32[1152]{0:T(1024)S(1)}, f32[1152]{0:T(1024)S(1)}, u32[]{:S(2)}, u32[]{:S(2)}) collective-permute-start(f32[1152]{0:T(1024)S(1)} %broadcast_multiply_fusion), channel_id=1, source_target_pairs={{0,0},{1,4},{4,1},{5,5},{2,2},{3,6},{6,3},{7,7},{8,8},{9,12},{12,9... | collective-permute-start | bytes 13832 | tf_op jit(solution)/shard_map/ppermute | solution.py:108
  (13 other events, 96.4 us)
Sparse Core Ops, SparseCore 0:
  25.8 48.8 all-gather.1
  91.8 47.0 reduce-scatter.1

commit v2 on v1

v2 whole, which is shorter than its diff:
```python
import jax
import jax.numpy as jnp
from jax import lax
from jax.experimental import pallas as pl
from jax.experimental.pallas import tpu as pltpu
from jax.sharding import Mesh, PartitionSpec as P

coef = 0.7978845608
f32, bf16 = jnp.float32, jnp.bfloat16

SLOTS = (0, 1, 3, 2)
PAD = 40
VMEM = pltpu.CompilerParams(vmem_limit_bytes=56 * 1024 * 1024)


def shift(block, axis, distance):
    size = lax.axis_size(axis)
    return lax.ppermute(block, axis, [(i, (i + distance) % size) for i in range(size)])


def pick(flag, a, b):
    return jnp.where(flag == 0, a, b), jnp.where(flag == 0, b, a)


def ring_gather(block, axis):
    size, r = lax.axis_size(axis), block.shape[0]
    me = lax.axis_index(axis)
    out = jnp.zeros((size * r, block.shape[1]), block.dtype)
    out = lax.dynamic_update_slice(out, block, (me * r, 0))
    right = left = block
    for k in range(1, size // 2 + 1):
        right = shift(right, axis, 1)
        out = lax.dynamic_update_slice(out, right, ((me - k) % size * r, 0))
        if k < size - k:
            left = shift(left, axis, -1)
            out = lax.dynamic_update_slice(out, left, ((me + k) % size * r, 0))
    return out


def direct_gather(block, axis):
    size = lax.axis_size(axis)
    me = lax.axis_index(axis)
    out = jnp.zeros((size,) + block.shape, block.dtype)
    out = lax.dynamic_update_index_in_dim(out, block, me, 0)
    for k in range(1, size):
        got = shift(block, axis, k)
        out = lax.dynamic_update_index_in_dim(out, got, (me - k) % size, 0)
    return out


def dot(a, b, ca=1, cb=0):
    return lax.dot_general(a, b, (((ca,), (cb,)), ((), ())), preferred_element_type=f32)


def tiles(width):
    starts = list(range(0, width - 255, 256))
    ends = starts[1:] + [width]
    return list(zip(starts, ends))


def up_kernel(scaled, first, grads_t, slope, out_term):
    for a, b in tiles(first.shape[1]):
        pre = dot(scaled[...], first[:, a:b])
        th = jnp.tanh(coef * (pre + 0.044715 * pre * pre * pre))
        slope[:, a:b] = 0.5 * (1.0 + th) + 0.5 * pre * (1.0 - th * th) * coef * (
            1.0 + 0.134145 * pre * pre
        )
        hidden = (0.5 * pre * (1.0 + th)).astype(bf16)
        out_term[:, a:b] = dot(grads_t[...], hidden).astype(bf16)


def down_kernel(grads, s0, s1, s2, s3, slope, scaled_t, dpre, o0, o1, o2, o3, second, sem):
    rows = s0.shape[0]
    copies = [
        pltpu.make_async_copy(s, second.at[pl.ds(rows * j, rows)], sem.at[j])
        for j, s in enumerate((s0, s1, s2, s3))
    ]
    for copy in copies:
        copy.start()
    for copy in copies:
        copy.wait()
    for a, b in tiles(second.shape[1]):
        part = (dot(grads[...], second[:, a:b]) * slope[:, a:b]).astype(bf16)
        dpre[:, a:b] = part
        for j, out in enumerate((o0, o1, o2, o3)):
            out[:, a:b] = dot(scaled_t[rows * j : rows * (j + 1)], part).astype(bf16)


def up(scaled, first, grads_t):
    t, d = scaled.shape
    half = first.shape[1]
    return pl.pallas_call(
        up_kernel,
        out_shape=(
            jax.ShapeDtypeStruct((t, half), f32),
            jax.ShapeDtypeStruct((d, half), bf16),
        ),
        compiler_params=VMEM,
        cost_estimate=pl.CostEstimate(
            flops=4 * t * d * half, bytes_accessed=4 * d * half, transcendentals=t * half
        ),
    )(scaled, first, grads_t)


def down(grads, slots, slope, scaled_t):
    t, wide = grads.shape
    rows, half = slots[0].shape
    whole = pl.BlockSpec(memory_space=pltpu.VMEM)
    away = pl.BlockSpec(memory_space=pl.ANY)
    return pl.pallas_call(
        down_kernel,
        out_shape=(jax.ShapeDtypeStruct((t, half), bf16),)
        + (jax.ShapeDtypeStruct((rows, half), bf16),) * 4,
        in_specs=[whole] + [away] * 4 + [whole] * 2,
        out_specs=(whole,) * 5,
        scratch_shapes=[pltpu.VMEM((wide, half), bf16), pltpu.SemaphoreType.DMA((4,))],
        compiler_params=VMEM,
        cost_estimate=pl.CostEstimate(
            flops=4 * t * wide * half, bytes_accessed=4 * wide * half, transcendentals=0
        ),
    )(grads, *slots, slope, scaled_t)


def turned(matrix, x, nz, nx):
    t, d = matrix.shape
    rows = d // (nz * nx)
    blocks = matrix.T.reshape(nz, nx, rows, t)
    blocks = jnp.stack(
        [lax.dynamic_index_in_dim(blocks, (x + o) % nx, 1, keepdims=False) for o in SLOTS]
    )
    blocks = jnp.pad(blocks, ((0, 0), (0, 0), (0, PAD - rows), (0, 0)))
    return blocks.reshape(nx * nz * PAD, t)


def local(nz, nx, acts, grad_in, gain, w_in, w_out):
    x, y = lax.axis_index("x"), lax.axis_index("y")
    rows, hid = w_in.shape[1:]
    half = hid // 2
    tokens, d = acts.shape[1:]
    scale = 1.0 / jnp.sqrt(jnp.float32(tokens * nz * nx * 2))

    both = jnp.concatenate([w_in, w_out], axis=0)
    mine, theirs = pick(y, both[:, :, :half], both[:, :, half:])
    top, bottom = pick(y, mine, shift(theirs, "y", 1))
    shard = jnp.concatenate([top, bottom], axis=1)
    first = direct_gather(shard[0], "x").reshape(nx * 2 * rows, half)
    first = lax.all_gather(first, "z", axis=0, tiled=True)
    second = ring_gather(jnp.pad(shard[1], ((0, PAD - 2 * rows), (0, 0))), "z")
    slots = [second] + [shift(second, "x", -o) for o in SLOTS[1:]]

    source = acts[0].astype(f32)
    centred = source - jnp.mean(source, axis=1, keepdims=True)
    inv = 1.0 / jnp.sqrt(jnp.mean(centred * centred, axis=1, keepdims=True) + 1e-06)
    normed = centred * inv
    scaled = (normed * gain[0][None, :]).astype(bf16)
    scaled = jnp.concatenate([scaled, shift(scaled, "y", 1)], axis=0)
    grads = jnp.concatenate([grad_in[0], shift(grad_in[0], "y", 1)], axis=0)
    scaled_t = turned(scaled, x, nz, nx)
    grads_w = turned(grads, x, nz, nx).T

    slope, out_term = up(scaled, first, grads.T)
    sum_out = lax.psum_scatter(out_term, "z", scatter_dimension=0, tiled=True)
    sum_out = sum_out.reshape(nx, 2 * rows, half)
    total_out = lax.dynamic_index_in_dim(sum_out, x, 0, keepdims=False).astype(f32)
    for o in SLOTS[1:]:
        part = lax.dynamic_index_in_dim(sum_out, (x + o) % nx, 0, keepdims=False)
        total_out += shift(part, "x", o).astype(f32)

    def returned(total, extra):
        total = total * scale
        keep, send = pick(y, total[:rows], total[rows:])
        if extra is not None:
            send = jnp.concatenate([send, extra], axis=0)
        got = shift(send, "y", 1)
        low, high = pick(y, keep, got[:rows])
        return jnp.concatenate([low, high], axis=1), got[rows:]

    grad_out, _ = returned(total_out, None)

    dpre, *terms = down(grads_w, slots, slope, scaled_t)
    total_in = terms[0].astype(f32)
    for o, term in zip(SLOTS[1:], terms[1:]):
        total_in += shift(term, "x", o).astype(f32)

    partial = dot(dpre, first, 1, 1)
    dscaled = partial[:tokens] + shift(partial[tokens:].astype(bf16), "y", 1).astype(f32)
    grad_g = jnp.sum(dscaled * normed, axis=0, keepdims=True) * scale
    dnormed = dscaled * gain[0][None, :]
    grad_x = grad_in[0].astype(f32) + inv * (
        dnormed
        - jnp.mean(dnormed, axis=1, keepdims=True)
        - normed * jnp.mean(dnormed * normed, axis=1, keepdims=True)
    )
    route = [(2 * h + c, (2 * h + c - 1) % 4) for h in range(2) for c in range(2)]
    handed = lax.ppermute(grad_x.astype(bf16), ("h", "c"), route)

    grad_g = sum([shift(grad_g, "x", o) for o in SLOTS[1:]], grad_g)
    upper = grad_g.astype(bf16)
    lower = (grad_g - upper.astype(f32)).astype(bf16)
    spare = jnp.concatenate([upper, lower], axis=0)
    spare = jnp.pad(spare, ((0, 0), (0, 2 * half - d))).reshape(4, half)
    spare = jnp.broadcast_to(spare[None], (nz, 4, half))
    total_in = total_in.reshape(nz, PAD, half)[:, : 2 * rows].astype(bf16)
    total_in = lax.all_to_all(jnp.concatenate([total_in, spare], axis=1), "z", 0, 0)
    total_in = jnp.sum(total_in.astype(f32), axis=0)
    gain_rows = total_in[2 * rows : 2 * rows + 2] + total_in[2 * rows + 2 :]
    grad_inw, gain_other = returned(total_in[: 2 * rows], gain_rows)
    grad_g = (gain_rows + gain_other).reshape(1, 2 * half)[:, :d]
    return handed[None], grad_inw[None], grad_out[None], grad_g


def solution(mesh):
    nz, nx = 8, mesh.shape["dp"] // 16
    fine = Mesh(mesh.devices.reshape(nz, nx, 2, 2, 2), ("z", "x", "y", "h", "c"))
    wide = P(("h", "c"), ("z", "x", "y"), None)
    slim = P(("h", "c"), None)

    def run(*args):
        return local(nz, nx, *args)

    return jax.shard_map(
        run,
        mesh=fine,
        in_specs=(wide, wide, slim, wide, wide),
        out_specs=(wide, wide, wide, slim),
        check_vma=False,
    )
```

time: 326 us -> 210 us (0.64); the launches traced: 320 us -> 209 us
  blocking collectives: 155 us -> 0 us
  waiting for transfers between devices: 43.8 us -> 80.9 us
  Pallas kernels: 0 us -> 20.1 us
  matrix products: 17.5 us -> 2.99 us
  other arithmetic: 5.68 us -> 18.4 us
  starting transfers between devices: 56.2 us -> 46.2 us
    psum x1 -> x0, blocking collectives: 125 us -> none  [local(): lax.psum(jnp.sum(dscaled * normed, axis=0), ('z', 'x', 'c')) * scale]
    all_gather x1 -> x0, blocking collectives: 30.2 us -> none  [local(): second = lax.all_gather(shard[1], 'z', axis=0, tiled=False)]
    ppermute x9 -> x1, starting transfers between devices: 27.2 us -> 0.01 us  [local(): handed = lax.ppermute(grad_x.astype(bf16), ('h', 'c'), route)]
    ppermute x15 -> x28, waiting for transfers between devices: 37.3 us -> 62.2 us  [shift(): lax.ppermute(block, axis, [(i, (i + distance) % size) for i in range(size)])]
    pallas_call x0 -> x2, Pallas kernels: none -> 20.1 us  [the longest x1 10.1 us: up(): pl.pallas_call(up_kernel, out_shape=(jax.ShapeDtypeStruct((t, half), f32)...]
    all_to_all x1, waiting for transfers between devices: 0.01 us -> 18.7 us  [local(): lax.all_to_all(jnp.concatenate([total_in, spare], axis=1), 'z', 0, 0)]
    ppermute x15 -> x28, starting transfers between devices: 23.8 us -> 40.2 us  [shift(): lax.ppermute(block, axis, [(i, (i + distance) % size) for i in range(size)])]
    dot_general x5 -> x1, matrix products: 17.5 us -> 2.99 us  [dot(): lax.dot_general(a, b, (((ca,), (cb,)), ((), ())), preferred_element_type=...]
  transfers between devices with their start and end apart: 27 -> 32, of which waited for: 9 -> 15; matrix products, arithmetic and copies ran while one was open for 13% -> 18% of each run, Pallas kernels for 0% -> 5%
where the time goes in v2:
time: 210 us; the launch traced here: 209 us
  waiting for transfers between devices  80.9 us (39%)
  starting transfers between devices  46.2 us (22%)
  local copies, waits for them, and re-layouts  26 us (12%)
  Pallas kernels  20.1 us (10%)
  other arithmetic  18.4 us (9%)
  between operations  14.4 us (7%)
  matrix products  2.99 us (1%)
    ppermute x28, waiting for transfers between devices, shift(): lax.ppermute(block, axis, [(i, (i + distance) % size) for i in range(size)])  62.2 us
    ppermute x28, starting transfers between devices, shift(): lax.ppermute(block, axis, [(i, (i + distance) % size) for i in range(size)])  40.2 us
    all_to_all x1, waiting for transfers between devices, local(): lax.all_to_all(jnp.concatenate([total_in, spare], axis=1), 'z', 0, 0)  18.7 us
    pallas_call x1, Pallas kernels, up(): pl.pallas_call(up_kernel, out_shape=(jax.ShapeDtypeStruct((t, half), f32)...  10.1 us
    pallas_call x1, Pallas kernels, down(): pl.pallas_call(down_kernel, out_shape=(jax.ShapeDtypeStruct((t, half), bf...  9.99 us
    all_to_all x1, starting transfers between devices, local(): lax.all_to_all(jnp.concatenate([total_in, spare], axis=1), 'z', 0, 0)  5.89 us
    unnamed x26, local copies, waits for them, and re-layouts  5.02 us
    transpose x2, other arithmetic, turned(): blocks = matrix.T.reshape(nz, nx, rows, t)  4.86 us
  transfers between devices with their start and end apart: 32, of which 15 were waited for; matrix products, arithmetic and copies ran while one was open for 18% of the time, Pallas kernels for 5%

profile of v2, /device:TPU:10, one launch (start us, length us, event | category | flops | bytes accessed | tf_op | source)
XLA Modules:
  0.0 209.1 jit_solution(12976506976514273498)
XLA Ops:
  9.7 4.3 %collective-permute-done.1 = bf16[2,18,1088]{2,1,0:T(8,128)(2,1)S(1)} collective-permute-done((bf16[2,18,1088]{2,1,0:T(8,128)(2,1)S(1)}, bf16[2,18,1088]{2,1,0:T(8,128)(2,1)S(1)}, u32[]{:S(2)}, u32[]{:S(2)}) %collective-permute-start.1) | collective-permute-done | bytes 78368 | tf_op jit(solution)/shard_map/ppermute | solution.py:18
  19.9 3.9 %collective-permute-done.14 = bf16[36,1088]{1,0:T(8,128)(2,1)S(1)} collective-permute-done((bf16[36,1088]{1,0:T(8,128)(2,1)S(1)}, bf16[36,1088]{1,0:T(8,128)(2,1)S(1)}, u32[]{:S(2)}, u32[]{:S(2)}) %collective-permute-start.14) | collective-permute-done | bytes 78368 | tf_op jit(solution)/shard_map/ppermute | solution.py:18
  28.5 3.9 %collective-permute-start.3 = (bf16[40,1088]{1,0:T(8,128)(2,1)S(1)}, bf16[40,1088]{1,0:T(8,128)(2,1)S(1)}, u32[]{:S(2)}, u32[]{:S(2)}) collective-permute-start(bf16[40,1088]{1,0:T(8,128)(2,1)S(1)} %get-tuple-element.53), channel_id=1, source_target_pairs={{0,224},{32,0},{64,32},{96,64},{128,96},{160,128},{192,160},{224,1... | collective-permute-start | bytes 261128 | tf_op jit(solution)/shard_map/ppermute | solution.py:18
  35.1 3.5 %collective-permute-start.5 = (bf16[40,1088]{1,0:T(8,128)(2,1)S(1)}, bf16[40,1088]{1,0:T(8,128)(2,1)S(1)}, u32[]{:S(2)}, u32[]{:S(2)}) collective-permute-start(bf16[40,1088]{1,0:T(8,128)(2,1)S(1)} %collective-permute-done.3), channel_id=1, source_target_pairs={{0,224},{32,0},{64,32},{96,64},{128,96},{160,128},{192,160},{224,1... | collective-permute-start | bytes 261128 | tf_op jit(solution)/shard_map/ppermute | solution.py:18
  43.1 3.7 %collective-permute-start.7 = (bf16[40,1088]{1,0:T(8,128)(2,1)S(1)}, bf16[40,1088]{1,0:T(8,128)(2,1)S(1)}, u32[]{:S(2)}, u32[]{:S(2)}) collective-permute-start(bf16[40,1088]{1,0:T(8,128)(2,1)S(1)} %collective-permute-done.5), channel_id=1, source_target_pairs={{0,224},{32,0},{64,32},{96,64},{128,96},{160,128},{192,160},{224,1... | collective-permute-start | bytes 261128 | tf_op jit(solution)/shard_map/ppermute | solution.py:18
  51.2 6.7 %collective-permute-done.8 = bf16[40,1088]{1,0:T(8,128)(2,1)S(1)} collective-permute-done((bf16[40,1088]{1,0:T(8,128)(2,1)S(1)}, bf16[40,1088]{1,0:T(8,128)(2,1)S(1)}, u32[]{:S(2)}, u32[]{:S(2)}) %collective-permute-start.8) | collective-permute-done | bytes 87072 | tf_op jit(solution)/shard_map/ppermute | solution.py:18
  62.5 2.2 %maximum_bitcast_fusion.grads_t = bf16[1152,512]{1,0:T(8,128)(2,1)} fusion(bf16[256,1152]{0,1:T(8,128)(2,1)} %collective-permute-done, bf16[256,1152]{0,1:T(8,128)(2,1)S(1)} %bitcast.86), kind=kLoop, calls=%fused_computation.36 | loop fusion | flops 2359296 | bytes 2359296 | tf_op jit(solution)/shard_map/transpose | solution.py:127
  66.9 2.6 %fusion.38 = (bf16[1152,512]{1,0:T(8,128)(2,1)}, bf16[512,1152]{0,1:T(8,128)(2,1)}) fusion(bf16[256,1152]{0,1:T(8,128)(2,1)} %collective-permute-done.12, bf16[256,1152]{0,1:T(8,128)(2,1)S(1)} %fusion.21), kind=kLoop, calls=%fused_computation.104 | loop fusion | flops 2359296 | bytes 3538944 | tf_op jit(solution)/shard_map/transpose | solution.py:127
  72.9 2.4 %copy.22.scaled = bf16[512,1152]{1,0:T(8,128)(2,1)} copy(bf16[512,1152]{0,1:T(8,128)(2,1)} %get-tuple-element.40) | data formatting | bytes 2359296 | tf_op jit(solution)/shard_map/concatenate | solution.py:156
  75.3 2.4 %copy.21 = bf16[1280,512]{0,1:T(8,128)(2,1)} copy(bf16[1280,512]{1,0:T(8,128)(2,1)} %bitcast.87) | data formatting | bytes 2621440 | tf_op jit(solution)/shard_map/reshape | solution.py:132
  79.0 10.1 %shard_map.84 = (f32[512,1088]{1,0:T(8,128)}, bf16[1152,1088]{1,0:T(8,128)(2,1)}) custom-call(bf16[512,1152]{1,0:T(8,128)(2,1)} %copy.22.scaled, bf16[1152,1088]{1,0:T(8,128)(2,1)} %all-gather.2.cloned.1.call-done.first, bf16[1152,512]{1,0:T(8,128)(2,1)} %maximum_bitcast_fusion.grads_t), custom_call_target="tpu_custom_call" | custom-call | flops 2566914048 | bytes 5013504 | tf_op jit(solution)/shard_map/pallas_call | solution.py:92
  89.2 10.0 %shard_map.85 = (bf16[512,1088]{1,0:T(8,128)(2,1)}, bf16[320,1088]{1,0:T(8,128)(2,1)}, bf16[320,1088]{1,0:T(8,128)(2,1)}, bf16[320,1088]{1,0:T(8,128)(2,1)}, bf16[320,1088]{1,0:T(8,128)(2,1)}) custom-call(bf16[512,1280]{1,0:T(8,128)(2,1)} %bitcast.89, bf16[320,1088]{1,0:T(8,128)(2,1)} %constant_dynamic-update-slice_fusion.3.s0, ...), custom_call_target="tpu_custom_call" | custom-call | flops 2852126720 | bytes 5570560 | tf_op jit(solution)/shard_map/pallas_call | solution.py:110
  99.2 3.0 %fusion.41 = f32[512,1152]{0,1:T(8,128)S(1)} fusion(bf16[512,1088]{1,0:T(8,128)(2,1)} %get-tuple-element.12, bf16[1152,1088]{1,0:T(8,128)(2,1)S(1)} %copy-done.9), kind=kOutput, calls=%fused_computation.107 | convolution fusion | flops 1283457024 | bytes 5980160 | tf_op jit(solution)/shard_map/dot_general | solution.py:52
  103.9 8.6 %collective-permute-done.16 = bf16[256,1152]{0,1:T(8,128)(2,1)S(1)} collective-permute-done((bf16[256,1152]{0,1:T(8,128)(2,1)S(1)}, bf16[256,1152]{0,1:T(8,128)(2,1)S(1)}, u32[]{:S(2)}, u32[]{:S(2)}) %collective-permute-start.16) | collective-permute-done | bytes 589856 | tf_op jit(solution)/shard_map/ppermute | solution.py:18
  115.0 2.6 %collective-permute-start.22 = (f32[1,1152]{1,0:T(1,128)}, f32[1,1152]{1,0:T(1,128)}, u32[]{:S(2)}, u32[]{:S(2)}) collective-permute-start(f32[1,1152]{1,0:T(1,128)} %mul.116), channel_id=1, source_target_pairs={{0,24},{8,0},{16,8},{24,16},{1,25},{9,1},{17,9},{25,17},{2,26},{10... | collective-permute-start | bytes 13832 | tf_op jit(solution)/shard_map/ppermute | solution.py:18
  119.3 2.5 %collective-permute-start.18 = (bf16[320,1088]{1,0:T(8,128)(2,1)}, bf16[320,1088]{1,0:T(8,128)(2,1)}, u32[]{:S(2)}, u32[]{:S(2)}) collective-permute-start(bf16[320,1088]{1,0:T(8,128)(2,1)} %get-tuple-element.14), channel_id=1, source_target_pairs={{0,8},{8,16},{16,24},{24,0},{1,9},{9,17},{17,25},{25,1},{2,10},{10... | collective-permute-start | bytes 2088968 | tf_op jit(solution)/shard_map/ppermute | solution.py:18
  126.1 20.5 %collective-permute-done.18 = bf16[320,1088]{1,0:T(8,128)(2,1)} collective-permute-done((bf16[320,1088]{1,0:T(8,128)(2,1)}, bf16[320,1088]{1,0:T(8,128)(2,1)}, u32[]{:S(2)}, u32[]{:S(2)}) %collective-permute-start.18) | collective-permute-done | bytes 696352 | tf_op jit(solution)/shard_map/ppermute | solution.py:18
  146.7 2.9 %collective-permute-done.20 = bf16[320,1088]{1,0:T(8,128)(2,1)} collective-permute-done((bf16[320,1088]{1,0:T(8,128)(2,1)}, bf16[320,1088]{1,0:T(8,128)(2,1)}, u32[]{:S(2)}, u32[]{:S(2)}) %collective-permute-start.20) | collective-permute-done | bytes 696352 | tf_op jit(solution)/shard_map/ppermute | solution.py:18
  152.8 5.9 %all-to-all-start = ((bf16[8,40,1088]{2,1,0:T(8,128)(2,1)}), bf16[8,40,1088]{2,1,0:T(8,128)(2,1)}, u32[]{:S(2)}, u32[]{:S(2)}) async-start(bf16[8,40,1088]{2,1,0:T(8,128)(2,1)} %pad_maximum_fusion.1), calls=%async_computation | async-start | bytes 1474560 | tf_op jit(solution)/shard_map/all_to_all | solution.py:204
  159.3 2.4 %fusion.26 = bf16[256,1152]{0,1:T(8,128)(2,1)} fusion(bf16[1,256,1152]{1,2,0:T(8,128)(2,1)S(1)} %copy.20, f32[256]{0:T(256)S(1)} %get-tuple-element.55, f32[256]{0:T(256)S(1)} %get-tuple-element.56, f32[1152]{0:T(1024)S(1)} %reduce.1, f32[256]{0:T(256)S(1)} %copy-done.7, f32[256]{0:T(256)S(1)} %copy-done.5, bf16[1,256,1152]{1,2,0:T(8,128)(2,1)S(1)} %copy.19, ...), kind=kLoop, calls=%fused_computation.31 | loop fusion | flops 3833856 | bytes 3547648 | tf_op jit(solution)/shard_map/convert_element_type | solution.py:195
  161.7 18.7 %all-to-all-done = bf16[8,40,1088]{2,1,0:T(8,128)(2,1)} async-done(((bf16[8,40,1088]{2,1,0:T(8,128)(2,1)}), bf16[8,40,1088]{2,1,0:T(8,128)(2,1)}, u32[]{:S(2)}, u32[]{:S(2)}) %all-to-all-start) | async-done | bytes 696352 | tf_op jit(solution)/shard_map/all_to_all | solution.py:204
  183.5 3.0 %collective-permute-done.24 = f32[20,1088]{1,0:T(8,128)S(1)} collective-permute-done((f32[20,1088]{1,0:T(8,128)S(1)}, f32[20,1088]{1,0:T(8,128)S(1)}, u32[]{:S(2)}, u32[]{:S(2)}) %collective-permute-start.24) | collective-permute-done | bytes 87072 | tf_op jit(solution)/shard_map/ppermute | solution.py:18
  192.7 3.1 %collective-permute-done.27 = bf16[36,1088]{1,0:T(8,128)(2,1)S(1)} collective-permute-done((bf16[36,1088]{1,0:T(8,128)(2,1)S(1)}, bf16[36,1088]{1,0:T(8,128)(2,1)S(1)}, u32[]{:S(2)}, u32[]{:S(2)}) %collective-permute-start.27) | collective-permute-done | bytes 78368 | tf_op jit(solution)/shard_map/ppermute | solution.py:18
  198.5 2.8 %collective-permute-done.28 = f32[18,1088]{1,0:T(8,128)S(1)} collective-permute-done((f32[18,1088]{1,0:T(8,128)S(1)}, f32[18,1088]{1,0:T(8,128)S(1)}, u32[]{:S(2)}, u32[]{:S(2)}) %collective-permute-start.28) | collective-permute-done | bytes 78368 | tf_op jit(solution)/shard_map/ppermute | solution.py:18
  (134 shorter events, 62.8 us)
Async XLA Ops:
  7.2 71.9 %all-gather.2.cloned.1.call-start = ((), (), s32[]{:S(2)}) async-start(), calls=%async_computation.2 | async-start | bytes 2985984 | tf_op jit(solution)/shard_map/all_gather | solution.py:147
  16.1 46.3 %collective-permute-start = (bf16[256,1152]{0,1:T(8,128)(2,1)S(1)}, bf16[256,1152]{0,1:T(8,128)(2,1)}, u32[]{:S(2)}, u32[]{:S(2)}) collective-permute-start(bf16[256,1152]{0,1:T(8,128)(2,1)S(1)} %bitcast.85), channel_id=1, source_target_pairs={{0,4},{4,0},{1,5},{5,1},{2,6},{6,2},{3,7},{7,3},{8,12},{12,8},{9,1... | collective-permute-start | bytes 1769480 | tf_op jit(solution)/shard_map/ppermute | solution.py:18
  16.9 6.9 %collective-permute-start.15 = (bf16[36,1088]{1,0:T(8,128)(2,1)S(1)}, bf16[36,1088]{1,0:T(8,128)(2,1)S(1)}, u32[]{:S(2)}, u32[]{:S(2)}) collective-permute-start(bf16[36,1088]{1,0:T(8,128)(2,1)S(1)} %get-tuple-element.50), channel_id=1, source_target_pairs={{0,24},{8,0},{16,8},{24,16},{1,25},{9,1},{17,9},{25,17},{2,26},{10... | collective-permute-start | bytes 235016 | tf_op jit(solution)/shard_map/ppermute | solution.py:18
  17.8 6.1 %collective-permute-start.14 = (bf16[36,1088]{1,0:T(8,128)(2,1)S(1)}, bf16[36,1088]{1,0:T(8,128)(2,1)S(1)}, u32[]{:S(2)}, u32[]{:S(2)}) collective-permute-start(bf16[36,1088]{1,0:T(8,128)(2,1)S(1)} %get-tuple-element.50), channel_id=1, source_target_pairs={{0,16},{8,24},{16,0},{24,8},{1,17},{9,25},{17,1},{25,9},{2,18},{10... | collective-permute-start | bytes 235016 | tf_op jit(solution)/shard_map/ppermute | solution.py:18
  24.7 161.9 %reduce-scatter.2.cloned.1.call-start = ((), (), s32[]{:S(2)}) async-start(), calls=%async_computation.3 | async-start | bytes 2985984 | tf_op jit(solution)/shard_map/reduce_scatter | solution.py:162
  26.8 8.3 %collective-permute-start.2 = (bf16[40,1088]{1,0:T(8,128)(2,1)S(1)}, bf16[40,1088]{1,0:T(8,128)(2,1)S(1)}, u32[]{:S(2)}, u32[]{:S(2)}) collective-permute-start(bf16[40,1088]{1,0:T(8,128)(2,1)S(1)} %get-tuple-element.53), channel_id=1, source_target_pairs={{0,32},{32,64},{64,96},{96,128},{128,160},{160,192},{192,224},{224... | collective-permute-start | bytes 261128 | tf_op jit(solution)/shard_map/ppermute | solution.py:18
  28.5 6.5 %collective-permute-start.3 = (bf16[40,1088]{1,0:T(8,128)(2,1)S(1)}, bf16[40,1088]{1,0:T(8,128)(2,1)S(1)}, u32[]{:S(2)}, u32[]{:S(2)}) collective-permute-start(bf16[40,1088]{1,0:T(8,128)(2,1)S(1)} %get-tuple-element.53), channel_id=1, source_target_pairs={{0,224},{32,0},{64,32},{96,64},{128,96},{160,128},{192,160},{224,1... | collective-permute-start | bytes 261128 | tf_op jit(solution)/shard_map/ppermute | solution.py:18
  32.7 34.3 %collective-permute-start.12 = (bf16[256,1152]{0,1:T(8,128)(2,1)S(1)}, bf16[256,1152]{0,1:T(8,128)(2,1)}, u32[]{:S(2)}, u32[]{:S(2)}) collective-permute-start(bf16[256,1152]{0,1:T(8,128)(2,1)S(1)} %fusion.21), channel_id=1, source_target_pairs={{0,4},{4,0},{1,5},{5,1},{2,6},{6,2},{3,7},{7,3},{8,12},{12,8},{9,1... | collective-permute-start | bytes 1769480 | tf_op jit(solution)/shard_map/ppermute | solution.py:18
  35.1 6.5 %collective-permute-start.4 = (bf16[40,1088]{1,0:T(8,128)(2,1)S(1)}, bf16[40,1088]{1,0:T(8,128)(2,1)S(1)}, u32[]{:S(2)}, u32[]{:S(2)}) collective-permute-start(bf16[40,1088]{1,0:T(8,128)(2,1)S(1)} %collective-permute-done.2), channel_id=1, source_target_pairs={{0,32},{32,64},{64,96},{96,128},{128,160},{160,192},{192,224},{224... | collective-permute-start | bytes 261128 | tf_op jit(solution)/shard_map/ppermute | solution.py:18
  35.1 8.0 %collective-permute-start.5 = (bf16[40,1088]{1,0:T(8,128)(2,1)S(1)}, bf16[40,1088]{1,0:T(8,128)(2,1)S(1)}, u32[]{:S(2)}, u32[]{:S(2)}) collective-permute-start(bf16[40,1088]{1,0:T(8,128)(2,1)S(1)} %collective-permute-done.3), channel_id=1, source_target_pairs={{0,224},{32,0},{64,32},{96,64},{128,96},{160,128},{192,160},{224,1... | collective-permute-start | bytes 261128 | tf_op jit(solution)/shard_map/ppermute | solution.py:18
  41.6 8.3 %collective-permute-start.6 = (bf16[40,1088]{1,0:T(8,128)(2,1)S(1)}, bf16[40,1088]{1,0:T(8,128)(2,1)S(1)}, u32[]{:S(2)}, u32[]{:S(2)}) collective-permute-start(bf16[40,1088]{1,0:T(8,128)(2,1)S(1)} %collective-permute-done.4), channel_id=1, source_target_pairs={{0,32},{32,64},{64,96},{96,128},{128,160},{160,192},{192,224},{224... | collective-permute-start | bytes 261128 | tf_op jit(solution)/shard_map/ppermute | solution.py:18
  43.1 7.4 %collective-permute-start.7 = (bf16[40,1088]{1,0:T(8,128)(2,1)S(1)}, bf16[40,1088]{1,0:T(8,128)(2,1)S(1)}, u32[]{:S(2)}, u32[]{:S(2)}) collective-permute-start(bf16[40,1088]{1,0:T(8,128)(2,1)S(1)} %collective-permute-done.5), channel_id=1, source_target_pairs={{0,224},{32,0},{64,32},{96,64},{128,96},{160,128},{192,160},{224,1... | collective-permute-start | bytes 261128 | tf_op jit(solution)/shard_map/ppermute | solution.py:18
  49.9 8.0 %collective-permute-start.8 = (bf16[40,1088]{1,0:T(8,128)(2,1)S(1)}, bf16[40,1088]{1,0:T(8,128)(2,1)S(1)}, u32[]{:S(2)}, u32[]{:S(2)}) collective-permute-start(bf16[40,1088]{1,0:T(8,128)(2,1)S(1)} %collective-permute-done.6), channel_id=1, source_target_pairs={{0,32},{32,64},{64,96},{96,128},{128,160},{160,192},{192,224},{224... | collective-permute-start | bytes 261128 | tf_op jit(solution)/shard_map/ppermute | solution.py:18
  58.5 30.7 %collective-permute-start.11 = (bf16[320,1088]{1,0:T(8,128)(2,1)}, bf16[320,1088]{1,0:T(8,128)(2,1)}, u32[]{:S(2)}, u32[]{:S(2)}) collective-permute-start(bf16[320,1088]{1,0:T(8,128)(2,1)} %constant_dynamic-update-slice_fusion.3.s0), channel_id=1, source_target_pairs={{0,16},{8,24},{16,0},{24,8},{1,17},{9,25},{17,1},{25,9},{2,18},{10... | collective-permute-start | bytes 2088968 | tf_op jit(solution)/shard_map/ppermute | solution.py:18
  60.4 28.8 %collective-permute-start.10 = (bf16[320,1088]{1,0:T(8,128)(2,1)}, bf16[320,1088]{1,0:T(8,128)(2,1)}, u32[]{:S(2)}, u32[]{:S(2)}) collective-permute-start(bf16[320,1088]{1,0:T(8,128)(2,1)} %constant_dynamic-update-slice_fusion.3.s0), channel_id=1, source_target_pairs={{0,8},{8,16},{16,24},{24,0},{1,9},{9,17},{17,25},{25,1},{2,10},{10... | collective-permute-start | bytes 2088968 | tf_op jit(solution)/shard_map/ppermute | solution.py:18
  61.0 28.2 %collective-permute-start.9 = (bf16[320,1088]{1,0:T(8,128)(2,1)}, bf16[320,1088]{1,0:T(8,128)(2,1)}, u32[]{:S(2)}, u32[]{:S(2)}) collective-permute-start(bf16[320,1088]{1,0:T(8,128)(2,1)} %constant_dynamic-update-slice_fusion.3.s0), channel_id=1, source_target_pairs={{0,24},{8,0},{16,8},{24,16},{1,25},{9,1},{17,9},{25,17},{2,26},{10... | collective-permute-start | bytes 2088968 | tf_op jit(solution)/shard_map/ppermute | solution.py:18
  102.3 10.2 %collective-permute-start.16 = (bf16[256,1152]{0,1:T(8,128)(2,1)S(1)}, bf16[256,1152]{0,1:T(8,128)(2,1)S(1)}, u32[]{:S(2)}, u32[]{:S(2)}) collective-permute-start(bf16[256,1152]{0,1:T(8,128)(2,1)S(1)} %slice.147), channel_id=1, source_target_pairs={{0,4},{4,0},{1,5},{5,1},{2,6},{6,2},{3,7},{7,3},{8,12},{12,8},{9,1... | collective-permute-start | bytes 1769480 | tf_op jit(solution)/shard_map/ppermute | solution.py:18
  115.0 6.8 %collective-permute-start.22 = (f32[1,1152]{1,0:T(1,128)}, f32[1,1152]{1,0:T(1,128)}, u32[]{:S(2)}, u32[]{:S(2)}) collective-permute-start(f32[1,1152]{1,0:T(1,128)} %mul.116), channel_id=1, source_target_pairs={{0,24},{8,0},{16,8},{24,16},{1,25},{9,1},{17,9},{25,17},{2,26},{10... | collective-permute-start | bytes 13832 | tf_op jit(solution)/shard_map/ppermute | solution.py:18
  119.3 27.3 %collective-permute-start.18 = (bf16[320,1088]{1,0:T(8,128)(2,1)}, bf16[320,1088]{1,0:T(8,128)(2,1)}, u32[]{:S(2)}, u32[]{:S(2)}) collective-permute-start(bf16[320,1088]{1,0:T(8,128)(2,1)} %get-tuple-element.14), channel_id=1, source_target_pairs={{0,8},{8,16},{16,24},{24,0},{1,9},{9,17},{17,25},{25,1},{2,10},{10... | collective-permute-start | bytes 2088968 | tf_op jit(solution)/shard_map/ppermute | solution.py:18
  121.8 24.8 %collective-permute-start.19 = (bf16[320,1088]{1,0:T(8,128)(2,1)}, bf16[320,1088]{1,0:T(8,128)(2,1)}, u32[]{:S(2)}, u32[]{:S(2)}) collective-permute-start(bf16[320,1088]{1,0:T(8,128)(2,1)} %get-tuple-element.15), channel_id=1, source_target_pairs={{0,24},{8,0},{16,8},{24,16},{1,25},{9,1},{17,9},{25,17},{2,26},{10... | collective-permute-start | bytes 2088968 | tf_op jit(solution)/shard_map/ppermute | solution.py:18
  121.8 27.7 %collective-permute-start.20 = (bf16[320,1088]{1,0:T(8,128)(2,1)}, bf16[320,1088]{1,0:T(8,128)(2,1)}, u32[]{:S(2)}, u32[]{:S(2)}) collective-permute-start(bf16[320,1088]{1,0:T(8,128)(2,1)} %get-tuple-element.16), channel_id=1, source_target_pairs={{0,16},{8,24},{16,0},{24,8},{1,17},{9,25},{17,1},{25,9},{2,18},{10... | collective-permute-start | bytes 2088968 | tf_op jit(solution)/shard_map/ppermute | solution.py:18
  152.8 27.6 %all-to-all-start = ((bf16[8,40,1088]{2,1,0:T(8,128)(2,1)}), bf16[8,40,1088]{2,1,0:T(8,128)(2,1)}, u32[]{:S(2)}, u32[]{:S(2)}) async-start(bf16[8,40,1088]{2,1,0:T(8,128)(2,1)} %pad_maximum_fusion.1), calls=%async_computation | async-start | bytes 1474560 | tf_op jit(solution)/shard_map/all_to_all | solution.py:204
  161.7 20.8 %collective-permute-start.17 = (bf16[256,1152]{0,1:T(8,128)(2,1)}, bf16[256,1152]{0,1:T(8,128)(2,1)S(1)}, u32[]{:S(2)}, u32[]{:S(2)}) collective-permute-start(bf16[256,1152]{0,1:T(8,128)(2,1)} %fusion.26), channel_id=1, source_target_pairs={{0,3},{1,0},{2,1},{3,2},{4,7},{5,4},{6,5},{7,6},{8,11},{9,8},{10,9... | collective-permute-start | bytes 1769480 | tf_op jit(solution)/shard_map/ppermute | solution.py:195
  189.6 6.2 %collective-permute-start.27 = (bf16[36,1088]{1,0:T(8,128)(2,1)S(1)}, bf16[36,1088]{1,0:T(8,128)(2,1)S(1)}, u32[]{:S(2)}, u32[]{:S(2)}) collective-permute-start(bf16[36,1088]{1,0:T(8,128)(2,1)S(1)} %get-tuple-element.42), channel_id=1, source_target_pairs={{0,16},{8,24},{16,0},{24,8},{1,17},{9,25},{17,1},{25,9},{2,18},{10... | collective-permute-start | bytes 235016 | tf_op jit(solution)/shard_map/ppermute | solution.py:18
  (18 other events, 268.1 us)
Sparse Core Ops, SparseCore 0:
  24.8 48.1 all-gather.1
  119.4 58.3 reduce-scatter.1
